TPU v7x, 32 devices: a whole 2x2x4 slice. The times are simulated.
32 devices in a mesh: ctx: 8 (over z, x), fsdp: 4 (over y, core).
Axes of the slice: x: 2, y: 2, z: 4, core: 2. Of those that a mesh axis runs over, the one named last changes fastest.
Arguments:
- query: bfloat16 [2048, 2048], P('ctx', 'fsdp'), may hold values from -11 to 11
- key: bfloat16 [2048, 2048], P('ctx', 'fsdp'), may hold values from -11 to 11
- value: bfloat16 [2048, 2048], P('ctx', 'fsdp'), may hold values from -6 to 6
- doc_ids: int32 [2048], P('ctx'), may hold values from 0 to 5, never falling along the last dimension, each value on 1 to 512 neighbouring positions
- out_weight: bfloat16 [2048, 4096], P(('fsdp', 'ctx')), may hold values from -0.125 to 0.125
- grad_out: bfloat16 [2048, 4096], P('ctx', 'fsdp'), may hold values from -6 to 6
Outputs:
- grad_query: bfloat16 [2048, 2048], P('ctx', 'fsdp')
- grad_key: bfloat16 [2048, 2048], P('ctx', 'fsdp')
- grad_value: bfloat16 [2048, 2048], P('ctx', 'fsdp')
- grad_out_weight: float32 [2048, 4096], P(('fsdp', 'ctx'))
Inputs may be any that keep to these rules, and one draw needn't show every extreme that they name: `doc_ids`: document ids never fall along the sequence; every document has 1 to 512 tokens and one has exactly 512.
All inputs are finite; a program needn't handle non-finite values.
Results may differ from a plain program's by a relative error of at most 0.034.
Values may be sent and summed in bfloat16 or wider, within the bound.
A program may use at most 128 MiB of HBM per device.

v0:
```python
import math

import jax
import jax.numpy as jnp
from jax import lax
from jax.experimental import pallas as pl
from jax.experimental.pallas import tpu as pltpu
from jax.sharding import PartitionSpec as P

DH = 128


NEGATIVE = -1e30


def shifted(array, axis, by):
    devices = lax.axis_size(axis)
    pairs = [(i, i + by) for i in range(devices) if 0 <= i + by < devices]
    return lax.ppermute(array, axis, pairs)


def as_sent(array):

    def short(part):
        return part.astype(jnp.bfloat16) if part.dtype == jnp.float32 else part

    return jax.tree.map(short, array)


def passed_along(block, axis, distance):
    devices = range(lax.axis_size(axis))
    route = [((i - distance) % len(devices), i) for i in devices]
    return lax.ppermute(block, axis, route)


def shards_general(query, key, value, doc_ids, out_weight, grad_out):
    tok_rows = query.shape[0]
    feature_width = query.shape[1]
    head_count = feature_width // DH
    cycle_size = lax.axis_size("ctx")
    cycle_reach = max(cycle_size // 8, 2)
    cycle_index = lax.axis_index("ctx")
    score_scale = 1.0 / math.sqrt(DH)
    local_pos = jnp.arange(tok_rows, dtype=jnp.int32)
    own_pos = cycle_index * tok_rows + local_pos
    own_docs = doc_ids + 1
    query_heads = query.reshape(tok_rows, head_count, DH)
    key_heads = key.reshape(tok_rows, head_count, DH)
    value_heads = value.reshape(tok_rows, head_count, DH)

    def scores_of(query_block, key_block):
        return (
            jnp.einsum("tnd,snd->nts", query_block, key_block, preferred_element_type=jnp.float32)
            * score_scale
        )

    state = (
        jnp.full((head_count, tok_rows), NEGATIVE, jnp.float32),
        jnp.zeros((head_count, tok_rows), jnp.float32),
        jnp.zeros((head_count, tok_rows, DH), jnp.float32),
    )
    key_block, value_block = (key_heads, value_heads)
    key_docs = own_docs
    stored_blocks = []
    for cycle_step in range(cycle_reach + 1):
        if cycle_step > 0:
            key_block, value_block = shifted((key_block, value_block), "ctx", 1)
            key_docs = shifted(key_docs, "ctx", 1)
        key_pos = own_pos - cycle_step * tok_rows
        pair_mask = (own_docs[:, None] == key_docs[None, :]) & (
            key_pos[None, :] <= own_pos[:, None]
        )
        forward_row_max, forward_row_sum, forward_output_sum = state
        forward_scores = jnp.where(pair_mask[None], scores_of(query_heads, key_block), NEGATIVE)
        new_max = jnp.maximum(forward_row_max, jnp.max(forward_scores, axis=-1))
        decay_factor = jnp.exp(forward_row_max - new_max)
        forward_weights = jnp.where(
            pair_mask[None], jnp.exp(forward_scores - new_max[..., None]), 0.0
        )
        new_sum = forward_row_sum * decay_factor + jnp.sum(forward_weights, axis=-1)
        weights_low = forward_weights.astype(jnp.bfloat16)
        new_output = forward_output_sum * decay_factor[..., None] + jnp.einsum(
            "nts,snd->ntd", weights_low, value_block, preferred_element_type=jnp.float32
        )
        state = (new_max, new_sum, new_output)
        stored_blocks.append((key_block, value_block, pair_mask))
    row_max, row_sum, output_sum = state
    log_total = row_max + jnp.log(row_sum)
    attn_heads = (output_sum / row_sum[..., None]).astype(jnp.bfloat16).transpose(1, 0, 2)
    attention = attn_heads.reshape(tok_rows, feature_width)
    grad_full = lax.all_gather(grad_out, "fsdp", axis=1, tiled=True)
    grad_attn = lax.dot_general(
        grad_full,
        lax.all_gather(out_weight, "ctx", axis=0, tiled=True),
        (((1,), (1,)), ((), ())),
        preferred_element_type=jnp.float32,
    ).astype(jnp.bfloat16)
    grad_weight = lax.psum_scatter(
        lax.dot_general(
            attention, grad_full, (((0,), (0,)), ((), ())), preferred_element_type=jnp.float32
        ),
        "ctx",
        scatter_dimension=0,
        tiled=True,
    )
    grad_heads = grad_attn.reshape(tok_rows, head_count, DH)
    delta_sum = jnp.einsum(
        "tnd,tnd->nt", grad_heads, attn_heads, preferred_element_type=jnp.float32
    )
    grad_query = jnp.zeros((tok_rows, head_count, DH), jnp.float32)
    carried = None
    for cycle_step in range(cycle_reach + 1):
        key_block, value_block, pair_mask = stored_blocks[cycle_step]
        if cycle_step > 0:
            carried = jax.tree.map(
                lambda part, own: part.astype(own.dtype),
                passed_along(as_sent(carried), "ctx", 1),
                carried,
            )
        scores = scores_of(query_heads, key_block)
        weights = jnp.where(pair_mask[None], jnp.exp(scores - log_total[..., None]), 0.0)
        rounded = weights.astype(jnp.bfloat16)
        value_part = jnp.einsum(
            "nts,tnd->snd", rounded, grad_heads, preferred_element_type=jnp.float32
        )
        grad_weights = jnp.einsum(
            "tnd,snd->nts", grad_heads, value_block, preferred_element_type=jnp.float32
        )
        grad_scores = (weights * (grad_weights - delta_sum[..., None])).astype(jnp.bfloat16)
        query_part = (
            jnp.einsum("nts,snd->tnd", grad_scores, key_block, preferred_element_type=jnp.float32)
            * score_scale
        )
        key_part = (
            jnp.einsum("nts,tnd->snd", grad_scores, query_heads, preferred_element_type=jnp.float32)
            * score_scale
        )
        query_part, key_part, value_part = (query_part, key_part, value_part)
        grad_query = grad_query + query_part
        if cycle_step == 0:
            carried = (key_part, value_part)
        else:
            carried = (carried[0] + key_part, carried[1] + value_part)
    grad_key, grad_value = jax.tree.map(
        lambda part, own: part.astype(own.dtype),
        passed_along(as_sent(carried), "ctx", -cycle_reach),
        carried,
    )
    return (
        grad_query.reshape(tok_rows, feature_width).astype(jnp.bfloat16),
        grad_key.reshape(tok_rows, feature_width).astype(jnp.bfloat16),
        grad_value.reshape(tok_rows, feature_width).astype(jnp.bfloat16),
        grad_weight,
    )


LINE = 4
F32 = jnp.float32
BF16 = jnp.bfloat16


def dot(a, b, dims):
    return lax.dot_general(a, b, (dims, ((), ())), preferred_element_type=F32)


def pair_kernel(
    q_ref, k_ref, v_ref, doc_ref, w_ref, g_ref,
    dq_ref, dk_ref, dv_ref, gw_ref,
    docs, kwin, vwin, dwin, wall, gall, attn_pair, probs_all, part, up_out, down_out, up_in, down_in,
    pair_out, pair_in, ga_own, ga_out, ga_in, own_grads, grads_out, grads_in,
    fold_in, fold_out,
    local_sem, wx_send, wx_recv, w_send, w_recv, g_send, g_fwd, g_recv, kv_send, kv_recv,
    kp_send, kp_fwd, kp_recv,
    at_send, at_recv, up_send, up_recv, down_send, down_recv, px_send, px_recv,
    ga_send, ga_recv, gr_send, gr_recv, fold_send, fold_recv,
):
    c = lax.axis_index("ctx")
    f = lax.axis_index("fsdp")
    z, x = c // 2, c % 2
    y, core = f // 2, f % 2
    rows = q_ref.shape[0]
    heads = q_ref.shape[1] // DH
    unit = w_ref.shape[0]
    width = g_ref.shape[1]
    scale = 1.0 / math.sqrt(DH)
    pending = []

    def remote(src, dst, ss, rs, dev):
        return pltpu.make_async_remote_copy(
            src_ref=src, dst_ref=dst, send_sem=ss, recv_sem=rs,
            device_id=dev, device_id_type=pl.DeviceIdType.MESH,
        )

    def send(src, dst, ss, rs, dev, cond=None):
        def start():
            remote(src, dst, ss, rs, dev).start()

        def finish():
            remote(src, dst, ss, rs, dev).wait_send()

        if cond is None:
            start()
        else:
            pl.when(cond)(start)
        pending.append((cond, finish))

    def arrived(dst, ss, rs):
        remote(dst, dst, ss, rs, (c, f)).wait_recv()

    pair = (c + 1 - 2 * x, f)
    up = (c + 2, f)
    down = (c - 2, f)
    has_up, has_down = z < LINE - 1, z > 0

    barrier = pltpu.get_barrier_semaphore()

    def greet(dev):
        pl.semaphore_signal(barrier, inc=1, device_id=dev, device_id_type=pl.DeviceIdType.MESH)

    greet(pair)
    greet((c, f + 1 - 2 * core))
    greet((c, f + 2 - 4 * y))
    greet((c + 1 - 2 * x, f + 2 - 4 * y))
    pl.when(has_up)(lambda: greet(up))
    pl.when(has_down)(lambda: greet(down))
    pl.semaphore_wait(barrier, 4 + (z + LINE - 1) // LINE + (2 * LINE - 2 - z) // LINE)

    docs[...] = jnp.broadcast_to(doc_ref[...], (8, rows))
    halfc = heads * DH // 2
    backward_order = 1 - z // 2
    backward_order_up = 1 - (z + 1) // 2
    first, second, last = (pl.ds(i * rows, rows) for i in range(3))

    def half_cols(i, backward):
        return pl.ds(pl.multiple_of((i + (1 - 2 * i) * backward) * halfc, halfc), halfc)

    send(docs, dwin.at[:, first], kv_send.at[2, 0], kv_recv.at[2, 0], up, has_up)
    send(docs, dwin.at[:, second], kp_send.at[2, 0], kp_recv.at[2, 0], pair, x == 0)
    for i in range(2):
        hu, hp = half_cols(i, backward_order_up), half_cols(i, backward_order)
        for n, (own, win) in enumerate(((k_ref, kwin), (v_ref, vwin))):
            send(own.at[:, hu], win.at[first, hu], kv_send.at[i, n], kv_recv.at[i, n], up, has_up)
            send(own.at[:, hp], win.at[second, hp], kp_send.at[i, n], kp_recv.at[i, n], pair, x == 0)

    mine = pl.ds(pl.multiple_of(x * unit, unit), unit)
    other = pl.ds(pl.multiple_of((1 - x) * unit, unit), unit)
    for j in range(2):
        cols = pl.ds(pl.multiple_of(2 * j * width + (1 - x) * width, width), width)
        send(
            w_ref.at[:, cols], wall.at[z, mine, pl.ds(j * width, width)],
            wx_send.at[j], wx_recv.at[j], pair,
        )
    local = []
    for j in range(2):
        cols = pl.ds(pl.multiple_of(2 * j * width + x * width, width), width)
        copy = pltpu.make_async_copy(
            w_ref.at[:, cols], wall.at[z, mine, pl.ds(j * width, width)], local_sem.at[j]
        )
        copy.start()
        local.append(copy)

    block = gall.at[
        pl.ds(pl.multiple_of(x * rows, rows), rows), pl.ds(pl.multiple_of(y * width, width), width)
    ]
    lead = core == x
    taker = 2 * z + core
    send(
        g_ref, block, g_send.at[0], g_recv.at[2 * x + y], (taker, 2 * (1 - y) + core)
    )
    send(
        g_ref, block, g_send.at[1], g_recv.at[2 * x + y], (taker, 2 * y + core), core != x
    )
    sibling = (c, f + 1 - 2 * core)

    @pl.when(lead)
    def _():
        pltpu.make_async_copy(g_ref, block, local_sem.at[2]).start()

    for copy in local:
        copy.wait()

    def spread(zb, rows_of, slot, rs, upward, downward):
        view = wall.at[zb, rows_of, :]
        if upward is not None:
            send(view, view, w_send.at[0, slot], rs, up, upward)
        if downward is not None:
            send(view, view, w_send.at[1, slot], rs, down, downward)

    spread(z, mine, 0, w_recv.at[z, x], None, has_down)
    for j in range(2):
        arrived(wall.at[z, other, pl.ds(j * width, width)], wx_send.at[j], wx_recv.at[j])
    spread(z, other, 1, w_recv.at[z, 1 - x], None, has_down)

    kwin[last, :] = k_ref[...]
    vwin[last, :] = v_ref[...]
    dwin[:, last] = docs[...]

    def nothing(slot):
        kwin[slot, :] = jnp.zeros((rows, heads * DH), BF16)
        vwin[slot, :] = jnp.zeros((rows, heads * DH), BF16)
        dwin[:, slot] = jnp.full((8, rows), -1, jnp.int32)

    pl.when(z == 0)(lambda: nothing(first))
    pl.when((z == 0) & (x == 0))(lambda: nothing(second))

    relay = (x == 1) & has_down

    def relayed(part_of, ss, rs, fs, ps):
        src = part_of(first)

        @pl.when(has_down)
        def _():
            arrived(src, ss, rs)

        send(src, part_of(second), fs, ps, pair, relay)

    def take(part_of, ss, ps):
        @pl.when((x == 1) | has_down)
        def _():
            arrived(part_of(second), ss, ps)

    def win_part(win, cols):
        return lambda slot: win.at[slot, cols]

    def doc_part(slot):
        return dwin.at[:, slot]

    relayed(doc_part, kv_send.at[2, 0], kv_recv.at[2, 0], kp_fwd.at[2, 0], kp_recv.at[2, 0])
    for i in range(2):
        for n, win in enumerate((kwin, vwin)):
            relayed(
                win_part(win, half_cols(i, backward_order)),
                kv_send.at[i, n], kv_recv.at[i, n], kp_fwd.at[i, n], kp_recv.at[i, n],
            )
    spread(z, mine, 0, w_recv.at[z, x], has_up, None)
    spread(z, other, 1, w_recv.at[z, 1 - x], has_up, None)

    for xs in range(2):
        for ys in range(2):
            s = 2 * xs + ys
            view = gall.at[pl.ds(xs * rows, rows), pl.ds(ys * width, width)]
            own = (x == xs) & (y == ys)

            @pl.when(lead & own)
            def _():
                pltpu.make_async_copy(g_ref, view, local_sem.at[2]).wait()

            @pl.when(lead & jnp.logical_not(own))
            def _():
                arrived(view, g_fwd.at[s], g_recv.at[s])

            send(view, view, g_fwd.at[s], g_recv.at[s], sibling, lead)

    for s in range(4):
        @pl.when(jnp.logical_not(lead))
        def _():
            arrived(
                gall.at[pl.ds((s // 2) * rows, rows), pl.ds((s % 2) * width, width)],
                g_fwd.at[s], g_recv.at[s],
            )

    take(doc_part, kp_send.at[2, 0], kp_recv.at[2, 0])

    def take_half(i):
        for n, win in enumerate((kwin, vwin)):
            take(
                win_part(win, half_cols(i, backward_order)), kp_send.at[i, n], kp_recv.at[i, n]
            )

    window = 3 * rows
    here = pl.ds(pl.multiple_of(x * rows, rows), rows)
    there = pl.ds(pl.multiple_of((1 - x) * rows, rows), rows)
    t_pos = lax.broadcasted_iota(jnp.int32, (rows, window), 0) + 2 * rows
    j_pos = lax.broadcasted_iota(jnp.int32, (rows, window), 1)
    doc_col = jnp.transpose(jnp.broadcast_to(doc_ref[...], (DH, rows)))[:, 0:1]
    mask = (doc_col == dwin[0:1, :]) & (j_pos <= t_pos)

    def head_of(i):
        return i + (heads - 1 - 2 * i) * backward_order

    def cols_of(i):
        return pl.ds(pl.multiple_of(head_of(i) * DH, DH), DH)

    def forward(i):
        hc = cols_of(i)
        scores = dot(q_ref[:, hc], kwin[:, hc], ((1,), (1,))) * scale
        scores = jnp.where(mask, scores, NEGATIVE)
        top = jnp.max(scores, axis=1, keepdims=True)
        weights = jnp.where(mask, jnp.exp(scores - top), 0.0)
        inverse = 1.0 / jnp.sum(weights, axis=1, keepdims=True)
        out = dot(weights.astype(BF16), vwin[:, hc], ((1,), (0,))) * inverse
        probs_all[head_of(i)] = weights * inverse
        attn_pair[here, hc] = out.astype(BF16)
        view = attn_pair.at[here, hc]
        send(view, view, at_send.at[i], at_recv.at[i], pair)

    def partial(i):
        arrived(attn_pair.at[there, cols_of(i)], at_send.at[i], at_recv.at[i])
        part[head_of(i)] = dot(attn_pair[:, cols_of(i)], gall[...], ((0,), (0,)))

    def w_round(r):
        for u in range(2):
            view_of = pl.ds(u * unit, unit)

            @pl.when(z - r >= 0)
            def _():
                arrived(wall.at[z - r, view_of, :], w_send.at[0, 2 * r + u], w_recv.at[z - r, u])

            if r < LINE - 1:
                spread(
                    z - r, view_of, 2 * r + u, w_recv.at[z - r, u], (z - r >= 0) & has_up, None
                )

            @pl.when(z + r < LINE)
            def _():
                arrived(wall.at[z + r, view_of, :], w_send.at[1, 2 * r + u], w_recv.at[z + r, u])

            if r < LINE - 1:
                send(
                    wall.at[z + r, view_of, :], wall.at[z + r, view_of, :],
                    w_send.at[1, 2 * r + u], w_recv.at[z + r, u], down, (z + r < LINE) & has_down,
                )

    def sum_step(s):
        b_up = LINE - 1 - s + z
        b_down = s - (LINE - 1) + z
        goes_up = (z <= s) & has_up
        goes_down = (LINE - 1 - z <= s) & has_down

        @pl.when(goes_up & jnp.logical_not(has_down))
        def _():
            up_out[s] = part[b_up].astype(BF16)

        @pl.when(goes_up & has_down)
        def _():
            arrived(up_in.at[b_up], up_send.at[s], up_recv.at[b_up])
            up_out[s] = (part[b_up] + up_in[b_up].astype(F32)).astype(BF16)

        send(up_out.at[s], up_in.at[b_up], up_send.at[s], up_recv.at[b_up], up, goes_up)

        @pl.when(goes_down & jnp.logical_not(has_up))
        def _():
            down_out[s] = part[b_down].astype(BF16)

        @pl.when(goes_down & has_up)
        def _():
            arrived(down_in.at[b_down], down_send.at[s], down_recv.at[b_down])
            down_out[s] = (part[b_down] + down_in[b_down].astype(F32)).astype(BF16)

        send(
            down_out.at[s], down_in.at[b_down], down_send.at[s], down_recv.at[b_down],
            down, goes_down,
        )

    take_half(0)
    forward(0)
    forward(1)
    partial(0)
    sum_step(0)
    take_half(1)
    forward(2)
    w_round(1)
    forward(3)
    partial(1)
    partial(2)
    partial(3)
    w_round(2)
    sum_step(1)
    w_round(3)

    for h in range(heads):
        ga = dot(gall[...], wall[h], ((1,), (1,)))
        ga_own[h] = ga
        ga_out[h] = ga_own[h, there, :].astype(BF16)
        send(ga_out.at[h], ga_in.at[h], ga_send.at[h], ga_recv.at[h], pair)

    sum_step(2)

    def fold(h):
        @pl.when((x == 0) | has_down)
        def _():
            arrived(fold_in.at[h], fold_send.at[h], fold_recv.at[h])

        @pl.when((x == 1) & has_down)
        def _():
            fold_out[h] = (grads_out[h, 1].astype(F32) + fold_in[h].astype(F32)).astype(BF16)

        send(
            fold_out.at[h], grads_in.at[h], gr_send.at[h, 1], gr_recv.at[h],
            down, (x == 1) & has_down,
        )

        @pl.when(x == 0)
        def _():
            own_grads[h] = own_grads[h] + fold_in[h].astype(F32)

    for h in range(heads):
        hc = pl.ds(h * DH, DH)
        arrived(ga_in.at[h], ga_send.at[h], ga_recv.at[h])
        ga = (ga_own[h, here, :] + ga_in[h].astype(F32)).astype(BF16)
        delta = jnp.sum(
            ga.astype(F32) * attn_pair[here, hc].astype(F32), axis=1, keepdims=True
        )
        probs = probs_all[h]
        grad_v = dot(probs.astype(BF16), ga, ((0,), (0,)))
        grad_p = dot(ga, vwin[:, hc], ((1,), (1,)))
        grad_s = (probs * (grad_p - delta)).astype(BF16)
        dq_ref[:, hc] = (dot(grad_s, kwin[:, hc], ((1,), (0,))) * scale).astype(BF16)
        grad_k = dot(grad_s, q_ref[:, hc], ((0,), (0,))) * scale
        grads_out[h, 0, :, pl.ds(0, DH)] = grad_k[rows:2 * rows].astype(BF16)
        grads_out[h, 0, :, pl.ds(DH, DH)] = grad_v[rows:2 * rows].astype(BF16)
        send(
            grads_out.at[h, 0], fold_in.at[h], fold_send.at[h], fold_recv.at[h],
            pair, (x == 1) | has_down,
        )
        grads_out[h, 1, :, pl.ds(0, DH)] = grad_k[0:rows].astype(BF16)
        grads_out[h, 1, :, pl.ds(DH, DH)] = grad_v[0:rows].astype(BF16)
        send(
            grads_out.at[h, 1], grads_in.at[h], gr_send.at[h, 0], gr_recv.at[h],
            down, (x == 0) & has_down,
        )
        own_grads[h, :, pl.ds(0, DH)] = grad_k[2 * rows:]
        own_grads[h, :, pl.ds(DH, DH)] = grad_v[2 * rows:]
        if h > 0:
            fold(h - 1)
    fold(heads - 1)

    @pl.when(has_down)
    def _():
        arrived(up_in.at[z], up_send.at[0], up_recv.at[z])
        part[z] = part[z] + up_in[z].astype(F32)

    @pl.when(has_up)
    def _():
        arrived(down_in.at[z], down_send.at[0], down_recv.at[z])
        part[z] = part[z] + down_in[z].astype(F32)

    pair_out[...] = part[z, other, :].astype(BF16)
    send(pair_out, pair_in, px_send, px_recv, pair)
    for xs in range(2):
        @pl.when(x == xs)
        def _():
            for j in range(2):
                gw_ref[:, pl.ds((2 * j + xs) * width, width)] = part[
                    z, pl.ds(xs * unit, unit), pl.ds(j * width, width)
                ]

    for h in range(heads):
        hc = pl.ds(h * DH, DH)
        @pl.when(has_up)
        def _():
            arrived(grads_in.at[h], gr_send.at[h, 0], gr_recv.at[h])
            own_grads[h] = own_grads[h] + grads_in[h].astype(F32)

        total = own_grads[h]
        dk_ref[:, hc] = total[:, :DH].astype(BF16)
        dv_ref[:, hc] = total[:, DH:].astype(BF16)

    arrived(pair_in, px_send, px_recv)
    for xs in range(2):
        @pl.when(x == xs)
        def _():
            for j in range(2):
                gw_ref[:, pl.ds((2 * j + 1 - xs) * width, width)] = pair_in[
                    :, pl.ds(j * width, width)
                ].astype(F32)

    for cond, finish in pending:
        if cond is None:
            finish()
        else:
            pl.when(cond)(finish)


def handed_on(*refs):
    copies = [pltpu.make_async_copy(refs[i], refs[4 + i], refs[8].at[i]) for i in range(4)]
    for copy in copies:
        copy.start()
    for copy in copies:
        copy.wait()


def shards_pairs(query, key, value, doc_ids, out_weight, grad_out):
    rows, cols = query.shape
    heads = cols // DH
    unit, feats = out_weight.shape
    width = grad_out.shape[1]
    half = 2 * width
    dma = pltpu.SemaphoreType.DMA
    vm = pl.BlockSpec(memory_space=pltpu.VMEM)
    hbm = pl.BlockSpec(memory_space=pl.ANY)
    shapes = (
        jax.ShapeDtypeStruct((rows, cols), BF16),
        jax.ShapeDtypeStruct((rows, cols), BF16),
        jax.ShapeDtypeStruct((rows, cols), BF16),
        jax.ShapeDtypeStruct((unit, feats), F32),
    )
    outs = pl.pallas_call(
        pair_kernel,
        out_shape=shapes,
        in_specs=[vm] * 6,
        out_specs=(vm,) * 4,
        scratch_shapes=[
            pltpu.VMEM((8, rows), jnp.int32),
            pltpu.VMEM((3 * rows, cols), BF16),
            pltpu.VMEM((3 * rows, cols), BF16),
            pltpu.VMEM((8, 3 * rows), jnp.int32),
            pltpu.VMEM((LINE, 2 * unit, half), BF16),
            pltpu.VMEM((2 * rows, half), BF16),
            pltpu.VMEM((2 * rows, cols), BF16),
            pltpu.VMEM((heads, rows, 3 * rows), F32),
            pltpu.VMEM((LINE, 2 * unit, half), F32),
            pltpu.VMEM((LINE - 1, 2 * unit, half), BF16),
            pltpu.VMEM((LINE - 1, 2 * unit, half), BF16),
            pltpu.VMEM((LINE, 2 * unit, half), BF16),
            pltpu.VMEM((LINE, 2 * unit, half), BF16),
            pltpu.VMEM((unit, half), BF16),
            pltpu.VMEM((unit, half), BF16),
            pltpu.VMEM((heads, 2 * rows, DH), F32),
            pltpu.VMEM((heads, rows, DH), BF16),
            pltpu.VMEM((heads, rows, DH), BF16),
            pltpu.VMEM((heads, rows, 2 * DH), F32),
            pltpu.VMEM((heads, 2, rows, 2 * DH), BF16),
            pltpu.VMEM((heads, rows, 2 * DH), BF16),
            pltpu.VMEM((heads, rows, 2 * DH), BF16),
            pltpu.VMEM((heads, rows, 2 * DH), BF16),
            dma((3,)),
            dma((2,)), dma((2,)),
            dma((2, 2 * LINE)), dma((LINE, 2)),
            dma((2,)), dma((4,)), dma((4,)),
            dma((3, 2)), dma((3, 2)),
            dma((3, 2)), dma((3, 2)), dma((3, 2)),
            dma((heads,)), dma((heads,)),
            dma((LINE,)), dma((LINE,)), dma((LINE,)), dma((LINE,)),
            dma, dma,
            dma((heads,)), dma((heads,)),
            dma((heads, 2)), dma((heads,)),
            dma((heads,)), dma((heads,)),
        ],
        compiler_params=pltpu.CompilerParams(
            collective_id=0, has_side_effects=True, vmem_limit_bytes=56 * 1024 * 1024
        ),
    )(query, key, value, doc_ids[None, :], out_weight, grad_out)
    return pl.pallas_call(
        handed_on,
        out_shape=shapes,
        in_specs=[hbm] * 4,
        out_specs=(hbm,) * 4,
        scratch_shapes=[dma((4,))],
    )(*outs)


def solution(mesh):
    return jax.shard_map(
        shards_pairs if mesh.shape["ctx"] == 8 and mesh.shape["fsdp"] == 4 else shards_general,
        mesh=mesh,
        in_specs=(
            P("ctx", "fsdp"),
            P("ctx", "fsdp"),
            P("ctx", "fsdp"),
            P("ctx"),
            P(("fsdp", "ctx"), None),
            P("ctx", "fsdp"),
        ),
        out_specs=(P("ctx", "fsdp"), P("ctx", "fsdp"), P("ctx", "fsdp"), P(("fsdp", "ctx"), None)),
        check_vma=False,
    )
```

profile of v0, /device:TPU:24, one launch (start us, length us, event | category | flops | bytes accessed | tf_op | source)
XLA Modules:
  0.0 149.6 jit_solution(3396274302255076493)
XLA Ops:
  0.6 92.2 %shard_map.93 = (bf16[256,512]{1,0:T(8,128)(2,1)}, bf16[256,512]{1,0:T(8,128)(2,1)}, bf16[256,512]{1,0:T(8,128)(2,1)}, f32[64,4096]{1,0:T(8,128)}) custom-call(bf16[256,512]{1,0:T(8,128)(2,1)} %q_ref.1, bf16[256,512]{1,0:T(8,128)(2,1)} %k_ref.1, bf16[256,512]{1,0:T(8,128)(2,1)} %v_ref.1, s32[1,256]{1,0:T(1,128)} %bitcast.1, bf16[64,4096]{1,0:T(8,128)(2,1)} %w_ref.1, ...), custom_call_target="tpu_custom_call" | custom-call | tf_op jit(solution)/shard_map/pallas_call | solution.py:598
  92.9 56.7 %shard_map.94 = (bf16[256,512]{1,0:T(8,128)(2,1)}, bf16[256,512]{1,0:T(8,128)(2,1)}, bf16[256,512]{1,0:T(8,128)(2,1)}, f32[64,4096]{1,0:T(8,128)}) custom-call(bf16[256,512]{1,0:T(8,128)(2,1)} %get-tuple-element.8.refs_0_, bf16[256,512]{1,0:T(8,128)(2,1)} %get-tuple-element.9.refs_1_, bf16[256,512]{1,0:T(8,128)(2,1)} %get-tuple-element.10.refs_2_, ...), custom_call_target="tpu_custom_call" | custom-call | tf_op jit(solution)/shard_map/pallas_call | solution.py:644
where the time goes:
time: 150 us
  Pallas kernels  149 us (99%)
    pallas_call x1, Pallas kernels, shards_pairs(): pl.pallas_call(pair_kernel, out_shape=shapes, in_specs=[vm] * 6, out_spec...  92.2 us
    pallas_call x1, Pallas kernels, shards_pairs(): pl.pallas_call(handed_on, out_shape=shapes, in_specs=[hbm] * 4, out_specs...  56.7 us

commit v1 on v0

--- a/solution.py
+++ b/solution.py
@@ -573,10 +573,15 @@
 
 
 def handed_on(*refs):
-    copies = [pltpu.make_async_copy(refs[i], refs[4 + i], refs[8].at[i]) for i in range(4)]
-    for copy in copies:
+    held, sems = refs[8:12], refs[12]
+    inward = [pltpu.make_async_copy(refs[i], held[i], sems.at[0, i]) for i in range(4)]
+    outward = [pltpu.make_async_copy(held[i], refs[4 + i], sems.at[1, i]) for i in range(4)]
+    for copy in inward:
         copy.start()
-    for copy in copies:
+    for i in range(4):
+        inward[i].wait()
+        outward[i].start()
+    for copy in outward:
         copy.wait()
 
 
@@ -646,7 +651,7 @@
         out_shape=shapes,
         in_specs=[hbm] * 4,
         out_specs=(hbm,) * 4,
-        scratch_shapes=[dma((4,))],
+        scratch_shapes=[pltpu.VMEM(shape.shape, shape.dtype) for shape in shapes] + [dma((2, 4))],
     )(*outs)
 
 

time: 150 us -> 95.6 us (0.64)
  Pallas kernels: 149 us -> 94.8 us
    pallas_call x1, Pallas kernels: 56.7 us -> 2.51 us  [shards_pairs(): pl.pallas_call(handed_on, out_shape=shapes, in_specs=[hbm] * 4, out_specs...]
where the time goes in v1:
time: 95.6 us; the launch traced here: 95.4 us
  Pallas kernels  94.8 us (99%)
    pallas_call x1, Pallas kernels, shards_pairs(): pl.pallas_call(pair_kernel, out_shape=shapes, in_specs=[vm] * 6, out_spec...  92.2 us
    pallas_call x1, Pallas kernels, shards_pairs(): pl.pallas_call(handed_on, out_shape=shapes, in_specs=[hbm] * 4, out_specs...  2.51 us

profile of v1, /device:TPU:24, one launch (start us, length us, event | category | flops | bytes accessed | tf_op | source)
XLA Modules:
  0.0 95.4 jit_solution(3431499468181106790)
XLA Ops:
  0.6 92.2 %shard_map.93 = (bf16[256,512]{1,0:T(8,128)(2,1)}, bf16[256,512]{1,0:T(8,128)(2,1)}, bf16[256,512]{1,0:T(8,128)(2,1)}, f32[64,4096]{1,0:T(8,128)}) custom-call(bf16[256,512]{1,0:T(8,128)(2,1)} %q_ref.1, bf16[256,512]{1,0:T(8,128)(2,1)} %k_ref.1, bf16[256,512]{1,0:T(8,128)(2,1)} %v_ref.1, s32[1,256]{1,0:T(1,128)} %bitcast.1, bf16[64,4096]{1,0:T(8,128)(2,1)} %w_ref.1, ...), custom_call_target="tpu_custom_call" | custom-call | tf_op jit(solution)/shard_map/pallas_call | solution.py:603
  92.9 2.5 %shard_map.94 = (bf16[256,512]{1,0:T(8,128)(2,1)}, bf16[256,512]{1,0:T(8,128)(2,1)}, bf16[256,512]{1,0:T(8,128)(2,1)}, f32[64,4096]{1,0:T(8,128)}) custom-call(bf16[256,512]{1,0:T(8,128)(2,1)} %get-tuple-element.8.refs_0_, bf16[256,512]{1,0:T(8,128)(2,1)} %get-tuple-element.9.refs_1_, bf16[256,512]{1,0:T(8,128)(2,1)} %get-tuple-element.10.refs_2_, ...), custom_call_target="tpu_custom_call" | custom-call | tf_op jit(solution)/shard_map/pallas_call | solution.py:649
